TPU v7x, 512 devices: a whole 4x4x16 slice. The times are simulated.
512 devices in a mesh: batch: 4 (over x_hi, core), space: 128 (over x_lo, z, y).
Axes of the slice: x: 4 (x_hi: 2, x_lo: 2; x = x_hi * 2 + x_lo), y: 4, z: 16, core: 2. Of those that a mesh axis runs over, the one named last changes fastest.
Arguments:
- inputs: bfloat16 [4, 128, 64, 64, 128], P('batch', 'space'), may hold values from -6 to 6
- cotangent: bfloat16 [4, 128, 64, 64, 128], P('batch', 'space'), may hold values from -6 to 6
- mode_weights: bfloat16 [256, 16, 64, 128], P('space'), may hold values from -1.5 to 1.5
Outputs:
- input_grad: bfloat16 [4, 128, 64, 64, 128], P('batch', 'space')
- weight_grad: float32 [256, 16, 64, 128], P('space')
All inputs are finite; a program needn't handle non-finite values.
Results may differ from a plain program's by a relative error of at most 0.015.
Values may be sent and summed in bfloat16 or wider, within the bound.
A program may use at most 64 MiB of HBM per device.

v0:
```python
import math

import jax
import jax.numpy as jnp
from jax import lax
from jax.sharding import PartitionSpec as P

C = 64
X = 64
Y = 128
Z = 128
MX = 16
MY = 16
MZ = 16


two_pi = 2.0 * math.pi


def side_by_side(arrays, axis, split_dim, concat_dim, along):
    both = jnp.concatenate(arrays, axis=along)
    whole, at, finished = (
        lax.all_to_all(both, axis, split_axis=split_dim, concat_axis=concat_dim, tiled=True),
        0,
        [],
    )
    for a in arrays:
        finished.append(lax.slice_in_dim(whole, at, at + a.shape[along], axis=along))
        at += a.shape[along]
    return tuple(finished)


def in_one_piece(arrays, axis, dim, along):
    widths = [a.shape[along] for a in arrays]
    both = jnp.concatenate(arrays, axis=along)
    whole = lax.all_gather(both, axis, axis=dim, tiled=True)
    return tuple(jnp.split(whole, [sum(widths[:k]) for k in range(1, len(widths))], axis=along))


def twiddles(wave_list, positions, length):
    product = wave_list[:, None] * positions[None, :] % length
    angles = two_pi / length * product.astype(jnp.float32)
    return (jnp.cos(angles), jnp.sin(angles))


def wave_pair(retained, length):
    return jnp.concatenate([jnp.arange(retained // 2), jnp.arange(length - retained // 2, length)])


def plane_spectrum(values, z_table, cos_x, sin_x, factor):
    lead_dims = values.shape[:-3]
    along_z = jnp.dot(values.reshape(-1, Z), z_table, preferred_element_type=jnp.float32)
    along_z = along_z.reshape(lead_dims + (C, X, 2 * MZ))
    first_term = jnp.einsum("kx,...cxm->...ckm", cos_x, along_z)
    second_term = jnp.einsum("kx,...cxm->...ckm", sin_x, along_z)
    real_part = (first_term[..., :MZ] + second_term[..., MZ:]) * factor
    imag_part = (first_term[..., MZ:] - second_term[..., :MZ]) * factor
    stacked = jnp.stack([real_part, imag_part], axis=-4)
    return stacked.reshape(lead_dims + (2, C, MX * MZ)).astype(jnp.bfloat16)


def modes_along_y(spectra, cos_y, sin_y):
    values_f = spectra.astype(jnp.float32)
    real_in = values_f[:, :, 0]
    imag_in = values_f[:, :, 1]
    real_out = jnp.einsum("ky,bycp->pbkc", cos_y, real_in) + jnp.einsum(
        "ky,bycp->pbkc", sin_y, imag_in
    )
    imag_out = jnp.einsum("ky,bycp->pbkc", cos_y, imag_in) - jnp.einsum(
        "ky,bycp->pbkc", sin_y, real_in
    )
    return jnp.stack([real_out, imag_out], axis=3)


def planes_along_y(mode_data, cos_y, sin_y):
    values_f = mode_data.astype(jnp.float32)
    real_in = values_f[:, :, :, 0]
    imag_in = values_f[:, :, :, 1]
    real_out = jnp.einsum("ky,pbkc->bycp", cos_y, real_in) - jnp.einsum(
        "ky,pbkc->bycp", sin_y, imag_in
    )
    imag_out = jnp.einsum("ky,pbkc->bycp", sin_y, real_in) + jnp.einsum(
        "ky,pbkc->bycp", cos_y, imag_in
    )
    return jnp.stack([real_out, imag_out], axis=2)


def plane_inverse(spectra, cos_x, sin_x, z_back):
    lead_dims = spectra.shape[:-3]
    values_f = spectra.astype(jnp.float32).reshape(lead_dims + (2, C, MX, MZ))
    real_in = values_f[..., 0, :, :, :]
    imag_in = values_f[..., 1, :, :, :]
    real_out = jnp.einsum("kx,...ckm->...cxm", cos_x, real_in) - jnp.einsum(
        "kx,...ckm->...cxm", sin_x, imag_in
    )
    imag_out = jnp.einsum("kx,...ckm->...cxm", sin_x, real_in) + jnp.einsum(
        "kx,...ckm->...cxm", cos_x, imag_in
    )
    joined = jnp.concatenate([real_out, imag_out], axis=-1)
    result = jnp.dot(joined.reshape(-1, 2 * MZ), z_back, preferred_element_type=jnp.float32)
    return result.reshape(lead_dims + (C, X, Z)).astype(jnp.bfloat16)


def split_cot(cot_modes):
    real_part = cot_modes[:, :, :, 0]
    imag_part = cot_modes[:, :, :, 1]
    return (
        jnp.concatenate([real_part, imag_part], axis=-1),
        jnp.concatenate([imag_part, -real_part], axis=-1),
    )


def weight_terms(input_modes, cot_modes):
    cot_one, cot_two = split_cot(cot_modes)
    first_term = jnp.einsum(
        "pbki,pbkj->pkij", input_modes[:, :, :, 0], cot_one, preferred_element_type=jnp.float32
    )
    second_term = jnp.einsum(
        "pbki,pbkj->pkij", input_modes[:, :, :, 1], cot_two, preferred_element_type=jnp.float32
    )
    return first_term + second_term


def local(inputs, cotangent, mode_weights):
    inv_scale = 1.0 / math.sqrt(X * Y * Z)
    cos_z, sin_z = twiddles(jnp.arange(MZ), jnp.arange(Z), Z)
    z_table = jnp.concatenate([cos_z.T, -sin_z.T], axis=1).astype(jnp.bfloat16)
    z_back = jnp.concatenate([cos_z, -sin_z], axis=0) * inv_scale
    cos_x, sin_x = twiddles(wave_pair(MX, X), jnp.arange(X), X)
    plain_z = jnp.full((MZ,), inv_scale, jnp.float32)
    weight_z = jnp.where(jnp.arange(MZ) == 0, 1.0, 2.0).astype(jnp.float32) * inv_scale
    input_spec = plane_spectrum(inputs, z_table, cos_x, sin_x, plain_z)
    cot_spec = plane_spectrum(cotangent, z_table, cos_x, sin_x, weight_z)
    y_waves = wave_pair(MY, Y)
    positions = jnp.arange(Y)
    cos_y, sin_y = twiddles(y_waves, positions, Y)
    moved_input, moved_cot = side_by_side((input_spec, cot_spec), "space", 4, 1, 0)
    input_modes = modes_along_y(moved_input, cos_y, sin_y)
    cot_modes = modes_along_y(moved_cot, cos_y, sin_y)
    input_modes = input_modes.astype(jnp.bfloat16)
    cot_modes = cot_modes.astype(jnp.bfloat16)
    all_input, all_cot = in_one_piece((input_modes, cot_modes), "batch", 1, 0)
    weight_grad = weight_terms(all_input, all_cot)
    cot_one, cot_two = split_cot(cot_modes)
    grad_real = jnp.einsum(
        "pbkj,pkij->pbki", cot_one, mode_weights, preferred_element_type=jnp.float32
    )
    grad_imag = jnp.einsum(
        "pbkj,pkij->pbki", cot_two, mode_weights, preferred_element_type=jnp.float32
    )
    mode_grad = jnp.stack([grad_real, grad_imag], axis=3).astype(jnp.bfloat16)
    plane_modes = planes_along_y(mode_grad, cos_y, sin_y).astype(jnp.bfloat16)
    back_spec = lax.all_to_all(plane_modes, "space", split_axis=1, concat_axis=4, tiled=True)
    input_grad = plane_inverse(back_spec, cos_x, sin_x, z_back)
    return (input_grad, weight_grad)


def solution(mesh):
    placed = (
        P("batch", "space", None, None, None),
        P("batch", "space", None, None, None),
        P("space", None, None, None),
    )
    return jax.shard_map(
        local,
        mesh=mesh,
        in_specs=placed,
        out_specs=(P("batch", "space", None, None, None), P("space", None, None, None)),
        check_vma=False,
    )
```

profile of v0, /device:TPU:1, one launch (start us, length us, event | category | flops | bytes accessed | tf_op | source)
XLA Modules:
  0.0 85.1 jit_solution(3247114187017242042)
XLA Ops:
  0.6 0.0 copy-start
  0.7 0.1 negate_convert_fusion
  0.7 1.1 %copy-done = bf16[1,1,64,64,128]{4,3,2,1,0:T(8,128)(2,1)S(1)} copy-done((bf16[1,1,64,64,128]{4,3,2,1,0:T(8,128)(2,1)S(1)}, bf16[1,1,64,64,128]{4,3,2,1,0:T(8,128)(2,1)}, u32[]{:S(2)}) %copy-start) | copy-done | bytes 1048600
  1.9 0.5 convolution_bitcast_fusion
  2.3 0.0 copy-start.1
  2.3 0.5 reshape.385
  2.9 0.1 pad_add_fusion.1
  3.0 0.6 convolution_bitcast_fusion.2
  3.5 0.6 convolution_bitcast_fusion.3
  4.1 0.0 copy-done.1
  4.1 0.5 convolution_bitcast_fusion.1
  4.6 0.5 reshape.383
  5.2 0.6 convolution_bitcast_fusion.4
  5.7 0.6 convolution_bitcast_fusion.5
  6.3 0.1 fusion.17
  6.6 0.1 maximum_maximum_fusion
  6.7 0.3 copy.77
  7.0 0.9 %reshape.404 = bf16[128,2,256]{2,1,0:T(2,128)(2,1)} reshape(bf16[256,2,1,2,64]{4,3,2,1,0:T(2,128)(2,1)S(1)} %bitcast.205) | data formatting | bytes 262144
  7.9 21.4 %all-to-all-start = ((bf16[128,2,256]{2,1,0:T(2,128)(2,1)}), bf16[128,2,256]{2,1,0:T(2,128)(2,1)S(1)}, u32[]{:S(2)}, u32[]{:S(2)}) async-start(bf16[128,2,256]{2,1,0:T(2,128)(2,1)} %reshape.404), calls=%async_computation | async-start | bytes 262144 | tf_op jit(solution)/shard_map/all_to_all | solution.py:23
  29.3 0.1 sine_negate_fusion
  29.4 15.5 %all-to-all-done = bf16[128,2,256]{2,1,0:T(2,128)(2,1)S(1)} async-done(((bf16[128,2,256]{2,1,0:T(2,128)(2,1)}), bf16[128,2,256]{2,1,0:T(2,128)(2,1)S(1)}, u32[]{:S(2)}, u32[]{:S(2)}) %all-to-all-start) | async-done | bytes 131104 | tf_op jit(solution)/shard_map/all_to_all | solution.py:23
  44.9 0.2 reshape.405
  45.1 0.2 copy.31
  45.3 0.0 copy-start.2
  45.3 0.2 fusion.34
  45.6 0.2 fusion.33
  45.8 0.2 fusion.32
  46.0 0.2 fusion.31
  46.3 0.2 fusion.8
  46.5 0.2 bitcast_negate_fusion
  46.8 0.1 maximum_bitcast_fusion.2
  46.9 0.0 copy-done.2
  46.9 0.4 fusion.41
  47.2 0.3 fusion.57
  47.5 0.2 fusion.65
  47.8 0.2 fusion.11
  48.0 0.2 fusion.12
  48.3 10.5 %all_gather.3 = bf16[4,4,16,2,64]{4,2,3,0,1:T(8,128)(2,1)S(1)} all-gather(bf16[4,1,16,2,64]{4,2,3,0,1:T(8,128)(2,1)S(1)} %copy.37), channel_id=1, replica_groups=mesh['batch'=4,'space'=128] {'batch'}, dimensions={1}, use_global_device_ids=true | all-gather | bytes 81920 | tf_op jit(solution)/shard_map/all_gather | solution.py:36
  58.8 0.4 fusion.39
  59.2 0.3 fusion.5
  59.4 0.3 fusion.6
  59.7 0.1 copy.32
  59.9 0.7 reshape.406
  60.6 6.1 %all-to-all-start.1 = ((bf16[128,2,128]{2,1,0:T(2,128)(2,1)}), bf16[128,2,128]{2,1,0:T(2,128)(2,1)S(1)}, u32[]{:S(2)}, u32[]{:S(2)}) async-start(bf16[128,2,128]{2,1,0:T(2,128)(2,1)} %reshape.406), calls=%async_computation.1 | async-start | bytes 131072 | tf_op jit(solution)/shard_map/all_to_all | solution.py:153
  66.8 0.4 fusion.24
  67.2 1.4 %convolution_add_fusion = f32[2,16,64,128]{3,2,1,0:T(8,128)} fusion(f32[2,16,64,128]{3,2,1,0:T(8,128)S(1)} %fusion.24, bf16[2,4,16,64]{3,1,2,0:T(4,128)(2,1)S(1)} %fusion.206, bf16[2,4,16,64]{3,1,2,0:T(4,128)(2,1)S(1)} %bitcast.210, bf16[2,4,16,1,64]{4,2,3,0,1:T(8,128)(2,1)S(1)} %get-tuple-element.6), kind=kOutput, calls=%fused_computation.4 | convolution fusion | flops 2424832 | bytes 2146304 | tf_op jit(solution)/shard_map/pbki,pbkj->pkij/dot_general | solution.py:118
  68.5 13.2 %all-to-all-done.1 = bf16[128,2,128]{2,1,0:T(2,128)(2,1)S(1)} async-done(((bf16[128,2,128]{2,1,0:T(2,128)(2,1)}), bf16[128,2,128]{2,1,0:T(2,128)(2,1)S(1)}, u32[]{:S(2)}, u32[]{:S(2)}) %all-to-all-start.1) | async-done | bytes 65568 | tf_op jit(solution)/shard_map/all_to_all | solution.py:153
  81.8 0.1 reshape.407
  81.9 0.1 bitcast_bitcast_fusion
  82.0 0.1 copy.33
  82.1 0.3 fusion.22
  82.4 0.3 fusion.23
  82.8 0.3 fusion.1
  83.1 0.3 fusion.2
  83.5 0.1 maximum_bitcast_fusion
  83.6 1.6 %fusion = bf16[1,1,64,64,128]{4,3,2,1,0:T(8,128)(2,1)} fusion(bf16[64,64,32]{1,0,2:T(8,128)(2,1)S(1)} %maximum_bitcast_fusion, f32[16,128]{1,0:T(8,128)S(1)} %get-tuple-element.24, f32[16,128]{1,0:T(8,128)S(1)} %get-tuple-element.25), kind=kOutput, calls=%fused_computation.3 | convolution fusion | flops 33562624 | bytes 1327104 | tf_op jit(solution)/shard_map/dot_general | solution.py:100
  (17 shorter events, 0.3 us)
Async XLA Ops:
  0.6 1.2 %copy-start = (bf16[1,1,64,64,128]{4,3,2,1,0:T(8,128)(2,1)S(1)}, bf16[1,1,64,64,128]{4,3,2,1,0:T(8,128)(2,1)}, u32[]{:S(2)}) copy-start(bf16[1,1,64,64,128]{4,3,2,1,0:T(8,128)(2,1)} %param.4) | copy-start | bytes 3145732
  2.3 1.8 %copy-start.1 = (bf16[1,1,64,64,128]{4,3,2,1,0:T(8,128)(2,1)S(1)}, bf16[1,1,64,64,128]{4,3,2,1,0:T(8,128)(2,1)}, u32[]{:S(2)}) copy-start(bf16[1,1,64,64,128]{4,3,2,1,0:T(8,128)(2,1)} %param.3) | copy-start | bytes 3145732
  7.9 37.0 %all-to-all-start = ((bf16[128,2,256]{2,1,0:T(2,128)(2,1)}), bf16[128,2,256]{2,1,0:T(2,128)(2,1)S(1)}, u32[]{:S(2)}, u32[]{:S(2)}) async-start(bf16[128,2,256]{2,1,0:T(2,128)(2,1)} %reshape.404), calls=%async_computation | async-start | bytes 262144 | tf_op jit(solution)/shard_map/all_to_all | solution.py:23
  45.3 1.6 %copy-start.2 = (bf16[2,16,64,128]{3,2,1,0:T(8,128)(2,1)S(1)}, bf16[2,16,64,128]{3,2,1,0:T(8,128)(2,1)}, u32[]{:S(2)}) copy-start(bf16[2,16,64,128]{3,2,1,0:T(8,128)(2,1)} %param.5) | copy-start | bytes 1572868
  60.6 21.2 %all-to-all-start.1 = ((bf16[128,2,128]{2,1,0:T(2,128)(2,1)}), bf16[128,2,128]{2,1,0:T(2,128)(2,1)S(1)}, u32[]{:S(2)}, u32[]{:S(2)}) async-start(bf16[128,2,128]{2,1,0:T(2,128)(2,1)} %reshape.406), calls=%async_computation.1 | async-start | bytes 131072 | tf_op jit(solution)/shard_map/all_to_all | solution.py:153
where the time goes:
time: 85.4 us; the launch traced here: 85.1 us
  waiting for transfers between devices  28.8 us (34%)
  starting transfers between devices  27.6 us (32%)
  matrix products  11.6 us (14%)
  blocking collectives  10.5 us (12%)
  local copies, waits for them, and re-layouts  5.07 us (6%)
  between operations  0.93 us (1%)
    all_to_all x1, starting transfers between devices, side_by_side(): lax.all_to_all(both, axis, split_axis=split_dim, concat_axis=concat_dim,...  21.4 us
    all_to_all x1, waiting for transfers between devices, side_by_side(): lax.all_to_all(both, axis, split_axis=split_dim, concat_axis=concat_dim,...  15.5 us
    all_to_all x1, waiting for transfers between devices, local(): lax.all_to_all(plane_modes, 'space', split_axis=1, concat_axis=4, tiled=T...  13.2 us
    all_gather x1, blocking collectives, in_one_piece(): whole = lax.all_gather(both, axis, axis=dim, tiled=True)  10.5 us
    all_to_all x1, starting transfers between devices, local(): lax.all_to_all(plane_modes, 'space', split_axis=1, concat_axis=4, tiled=T...  6.15 us
    unnamed x12, local copies, waits for them, and re-layouts  3.12 us
  transfers between devices with their start and end apart: 2, of which 2 were waited for; matrix products, arithmetic and copies ran while one was open for 2% of the time, Pallas kernels for 0%

commit v1 on v0

v1 whole, which is shorter than its diff:
```python
import math

import jax
import jax.numpy as jnp
import ml_dtypes
import numpy as np
from jax import lax
from jax.experimental import pallas as pl
from jax.experimental.pallas import tpu as pltpu
from jax.sharding import PartitionSpec as P

C, X, Y, Z = 64, 64, 128, 128
MX, MY, MZ = 16, 16, 16
XL, NZ, NY = 2, 16, 4
NG = XL * NY
NB = 4
MESH = pl.DeviceIdType.MESH
BF, F32 = jnp.bfloat16, jnp.float32

KX = np.concatenate([np.arange(MX // 2), np.arange(X - MX // 2, X)])
KY = np.concatenate([np.arange(MY // 2), np.arange(Y - MY // 2, Y)])
SCALE = 1.0 / math.sqrt(X * Y * Z)


def bf(a):
    return np.asarray(a, np.float64).astype(ml_dtypes.bfloat16)


def turns(k, n, length):
    a = 2.0 * math.pi * ((np.asarray(k)[:, None] * np.asarray(n)[None, :]) % length) / length
    return np.cos(a), np.sin(a)


def tables():
    eye8 = np.eye(8)
    cx, sx = turns(KX, np.arange(X), X)
    ex = np.stack([cx, -sx])
    e8 = np.einsum("pkx,cd->pkcdx", ex, eye8).reshape(2 * MX * 8, 8 * X)
    cz, sz = turns(np.arange(MZ), np.arange(Z), Z)
    tz = np.concatenate(
        [np.concatenate([cz, sz], 1), np.concatenate([-sz, cz], 1)], 0
    )
    a = np.where(np.arange(MZ) == 0, 1.0, 2.0)
    t_in = tz * SCALE
    t_cot = tz * SCALE * np.tile(a, 2)[:, None]
    one_g = np.eye(NG)
    one_e = np.eye(2)
    down, up = [], []
    for g in range(NG):
        cell = 64 * (g // NY) + NY * np.arange(NZ) + g % NY
        cy, sy = turns(KY, cell, Y)
        d = [
            np.einsum("kz,gh,ef->gkezhf", m, one_g, one_e).reshape(256, 256)
            for m in (cy, sy)
        ]
        down.append(np.concatenate([d[0], d[1]], 1))
        up.append(np.concatenate([d[0].T, -d[1].T], 1))
    kz_of = (np.arange(256) // 16 % 2) * 8 + np.arange(256) % 8
    zb = (
        np.concatenate(
            [
                np.concatenate([cz[kz_of], sz[kz_of]], 1),
                np.concatenate([-sz[kz_of], cz[kz_of]], 1),
            ],
            0,
        )
        * SCALE
    )
    return bf(e8), bf(t_in), bf(t_cot), bf(np.stack(down)), bf(np.stack(up)), bf(zb), bf(e8.T)


def swapped(v):
    lane = lax.broadcasted_iota(jnp.int32, v.shape, v.ndim - 1)
    r = pltpu.roll(v, 64, v.ndim - 1)
    return jnp.where(lane < 64, r, -r)


def nn(a, b):
    return lax.dot_general(a, b, (((1,), (0,)), ((), ())), preferred_element_type=F32)


def nt(a, b):
    return lax.dot_general(a, b, (((1,), (1,)), ((), ())), preferred_element_type=F32)


def spectrum(f_ref, sems, copies, e8_ref, t_ref, b_ref, out_ref):
    for i in range(4):
        copies[i].wait()
        lo = f_ref[16 * i : 16 * i + 8].reshape(512, 128)
        hi = f_ref[16 * i + 8 : 16 * i + 16].reshape(512, 128)
        o = nn(e8_ref[...], jnp.concatenate([lo, hi], axis=1)).reshape(32, 8, 256)
        o = jnp.concatenate([o[:, :, :128], o[:, :, 128:]], axis=1)
        b_ref[:, 16 * i : 16 * i + 16, :] = o.astype(BF)
    lane = lax.broadcasted_iota(jnp.int32, (16, 128), 1)
    left = lane < 64
    found = [None] * MX
    for j in range(4):
        re = b_ref[4 * j : 4 * j + 4].reshape(256, 128)
        im = b_ref[16 + 4 * j : 20 + 4 * j].reshape(256, 128)
        o = nt(t_ref[...], jnp.concatenate([re, im], axis=1))
        for h in range(2):
            r = o[:16, 128 * h : 128 * h + 128]
            m = o[16:, 128 * h : 128 * h + 128]
            found[4 * j + 2 * h] = jnp.where(left, r, pltpu.roll(m, 64, 1))
            found[4 * j + 2 * h + 1] = jnp.where(left, pltpu.roll(r, 64, 1), m)
    for z in range(NZ):
        k, h = z // 2, z % 2
        tile = jnp.concatenate(
            [found[k][8 * h : 8 * h + 8], found[8 + k][8 * h : 8 * h + 8]], axis=0
        )
        out_ref[z] = tile.astype(BF)


def main_kernel(
    in_hbm, cot_hbm, w_hbm, e8_hbm, tin_hbm, tcot_hbm, down_hbm, up_hbm,
    q_ref, wg_ref,
    cot_v, in_v, w_v, e8_v, tin_v, tcot_v, down_v, up_v, b_v,
    zs_c, zs_i, zr_c, zr_i, gs_c, gs_i, gr_c, gr_i, du_s, du_r, q_s,
    g_all, u_all,
    load_sem, send_sem, recv_sem,
):
    b = lax.axis_index("batch")
    s = lax.axis_index("space")
    x_lo, z, y = s // (NZ * NY), (s // NY) % NZ, s % NY
    g = x_lo * NY + y

    loads = []

    def load(src, dst):
        c = pltpu.make_async_copy(src, dst, load_sem.at[len(loads)])
        c.start()
        loads.append(c)
        return c

    e8_c = load(e8_hbm, e8_v)
    tcot_c = load(tcot_hbm, tcot_v)
    cot_c = [
        load(cot_hbm.at[0, 0, pl.ds(16 * i, 16)], cot_v.at[pl.ds(16 * i, 16)]) for i in range(4)
    ]
    tin_c = load(tin_hbm, tin_v)
    in_c = [
        load(in_hbm.at[0, 0, pl.ds(16 * i, 16)], in_v.at[pl.ds(16 * i, 16)]) for i in range(4)
    ]
    down_c = load(down_hbm.at[g], down_v)
    w_c = load(w_hbm, w_v)
    up_c = load(up_hbm.at[g], up_v)

    def z_peer(j):
        t = lax.rem(z + j, NZ)
        return t, (b, x_lo * (NZ * NY) + t * NY + y)

    def g_peer(j):
        t = lax.rem(g + j, NG)
        return t, (b, (t // NY) * (NZ * NY) + z * NY + t % NY)

    def b_peer(j):
        return (lax.rem(b + j, NB), s)

    z_order = sorted(range(1, NZ), key=lambda j: -min(j, NZ - j))

    barrier = pltpu.get_barrier_semaphore()
    peers = [z_peer(j)[1] for j in z_order]
    peers += [g_peer(j)[1] for j in range(1, NG)] + [b_peer(j) for j in range(1, NB)]
    for p in peers:
        pl.semaphore_signal(barrier, inc=1, device_id=p, device_id_type=MESH)

    e8_c.wait()
    tcot_c.wait()
    spectrum(cot_v, None, cot_c, e8_v, tcot_v, b_v, zs_c)
    tin_c.wait()
    spectrum(in_v, None, in_c, e8_v, tin_v, b_v, zs_i)
    pl.semaphore_wait(barrier, len(peers))

    def remote(src, dst, k, to):
        pltpu.make_async_remote_copy(
            src_ref=src, dst_ref=dst, send_sem=send_sem.at[k], recv_sem=recv_sem.at[k],
            device_id=to, device_id_type=MESH,
        ).start()

    def z_start(src, dst, k):
        for j in z_order:
            t, to = z_peer(j)
            remote(src.at[t], dst.at[z], k, to)
        pltpu.make_async_copy(src.at[z], dst.at[z], recv_sem.at[k]).start()

    def g_start(src, dst, k):
        for j in range(1, NG):
            t, to = g_peer(j)
            remote(src.at[t], dst.at[g], k, to)
        pltpu.make_async_copy(src.at[g], dst.at[g], recv_sem.at[k]).start()

    def arrived(dst, k):
        pltpu.make_async_copy(dst, dst, recv_sem.at[k]).wait()

    def along_y(table, v):
        v = v.astype(F32)
        both = jnp.concatenate([v.astype(BF), swapped(v).astype(BF)], axis=0)
        return nn(table[...], both)

    z_start(zs_c, zr_c, 0)
    z_start(zs_i, zr_i, 1)

    down_c.wait()
    arrived(zr_c, 0)
    gs_c[...] = along_y(down_v, zr_c[...].reshape(256, 128)).astype(BF).reshape(NG, 32, 128)
    g_start(gs_c, gr_c, 2)
    arrived(zr_i, 1)
    gs_i[...] = along_y(down_v, zr_i[...].reshape(256, 128)).astype(BF).reshape(NG, 32, 128)
    g_start(gs_i, gr_i, 3)

    w_c.wait()
    arrived(gr_c, 2)
    gm = jnp.sum(gr_c[...].astype(F32), axis=0)
    gm_b = gm.astype(BF)
    g_all[b] = gm_b
    gm_f = gm_b.astype(F32)
    both = jnp.concatenate([gm_b, swapped(gm_f).astype(BF)], axis=0)
    row = lax.broadcasted_iota(jnp.int32, (64, 128), 0) % 32
    lane = lax.broadcasted_iota(jnp.int32, (64, 128), 1)
    code = (row % 2) * 16 + row // 2 - lane // 64
    acc = jnp.zeros((64, 128), F32)
    for k in range(8):
        o = nt(both, w_v[k // 4, 4 * (k % 4) : 4 * (k % 4) + 4].reshape(256, 128))
        acc = acc + jnp.where(code == 4 * k, o[:, :128], 0.0)
        acc = acc + jnp.where(code == 4 * k + 2, o[:, 128:], 0.0)
    acc = acc + pltpu.roll(acc, 64, 1)
    du_s[...] = jnp.where(lane[:32] < 64, acc[:32], acc[32:]).astype(BF)
    for j in range(1, NG):
        remote(du_s, du_r.at[g], 4, g_peer(j)[1])
    pltpu.make_async_copy(du_s, du_r.at[g], recv_sem.at[4]).start()
    for j in range(1, NB):
        remote(g_all.at[b], g_all.at[b], 6, b_peer(j))

    arrived(gr_i, 3)
    u_all[b] = jnp.sum(gr_i[...].astype(F32), axis=0).astype(BF)
    for j in range(1, NB):
        remote(u_all.at[b], u_all.at[b], 7, b_peer(j))

    up_c.wait()
    arrived(du_r, 4)
    q_s[...] = along_y(up_v, du_r[...].reshape(256, 128)).astype(BF).reshape(NZ, 16, 128)
    z_start(q_s, q_ref, 5)

    arrived(g_all.at[pl.ds(0, NB - 1)], 6)
    arrived(u_all.at[pl.ds(0, NB - 1)], 7)
    gv = g_all[...].reshape(128, 128)
    rhs = jnp.concatenate([gv, swapped(gv.astype(F32)).astype(BF)], axis=0)
    ut = u_all[...].reshape(128, 128).astype(F32).T
    ut = jnp.concatenate([ut[:64], ut[64:]], axis=1).astype(BF)
    which = lax.broadcasted_iota(jnp.int32, (64, 256), 1) % 32
    for e in range(2):
        for k in range(4):
            lhs = jnp.concatenate(
                [jnp.where(which == 2 * (4 * k + i) + e, ut, jnp.zeros_like(ut)) for i in range(4)],
                axis=0,
            )
            wg_ref[e, 4 * k : 4 * k + 4] = nn(lhs, rhs).reshape(4, 64, 128)

    arrived(q_ref, 5)

    def left(src, k):
        pltpu.make_async_copy(src, src, send_sem.at[k]).wait()

    left(zs_c.at[pl.ds(0, NZ - 1)], 0)
    left(zs_i.at[pl.ds(0, NZ - 1)], 1)
    left(gs_c.at[pl.ds(0, NG - 1)], 2)
    left(gs_i.at[pl.ds(0, NG - 1)], 3)
    left(du_r.at[pl.ds(0, NG - 1)], 4)
    left(q_s.at[pl.ds(0, NZ - 1)], 5)
    left(g_all.at[pl.ds(0, NB - 1)], 6)
    left(u_all.at[pl.ds(0, NB - 1)], 7)


def inverse_kernel(q_ref, wg_ref, zb_ref, xb_ref, ig_hbm, wo_hbm, c_v, o_v, sems):
    wg_c = pltpu.make_async_copy(wg_ref, wo_hbm, sems.at[4])
    wg_c.start()
    qt = q_ref[...].reshape(256, 128).astype(F32).T
    qt = jnp.concatenate([qt[:64], qt[64:]], axis=1).astype(BF)
    at = lax.broadcasted_iota(jnp.int32, (64, 512), 1) % 256
    kx_of = (at // 8 % 2) * 8 + at // 32
    for j in range(4):
        lhs = jnp.concatenate(
            [jnp.where(kx_of == 4 * j + i, qt, jnp.zeros_like(qt)) for i in range(4)], axis=0
        )
        o = nn(lhs, zb_ref[...])
        c_v[4 * j : 4 * j + 4] = o[:, :128].reshape(4, 64, 128)
        c_v[16 + 4 * j : 20 + 4 * j] = o[:, 128:].reshape(4, 64, 128)
    outs = []
    for i in range(4):
        lo = c_v[:, 16 * i : 16 * i + 8].reshape(256, 128)
        hi = c_v[:, 16 * i + 8 : 16 * i + 16].reshape(256, 128)
        o = nn(xb_ref[...], jnp.concatenate([lo, hi], axis=1).astype(BF))
        o_v[16 * i : 16 * i + 8] = o[:, :128].reshape(8, 64, 128).astype(BF)
        o_v[16 * i + 8 : 16 * i + 16] = o[:, 128:].reshape(8, 64, 128).astype(BF)
        c = pltpu.make_async_copy(
            o_v.at[pl.ds(16 * i, 16)], ig_hbm.at[0, 0, pl.ds(16 * i, 16)], sems.at[i]
        )
        c.start()
        outs.append(c)
    for c in outs:
        c.wait()
    wg_c.wait()


def local(inputs, cotangent, mode_weights):
    e8, t_in, t_cot, down, up, zb, xb = (jnp.asarray(t) for t in tables())
    anyw = pl.BlockSpec(memory_space=pltpu.HBM)
    vmem = pl.BlockSpec(memory_space=pltpu.VMEM)
    dma = pltpu.SemaphoreType.DMA
    operands = (inputs, cotangent, mode_weights, e8, t_in, t_cot, down, up)
    q, wg = pl.pallas_call(
        main_kernel,
        out_shape=(
            jax.ShapeDtypeStruct((NZ, 16, 128), BF),
            jax.ShapeDtypeStruct((2, MY, C, 2 * C), F32),
        ),
        in_specs=[anyw] * 8,
        out_specs=(vmem, vmem),
        scratch_shapes=[
            pltpu.VMEM((C, X, Z), BF),
            pltpu.VMEM((C, X, Z), BF),
            pltpu.VMEM((2, MY, C, 2 * C), BF),
            pltpu.VMEM((256, 512), BF),
            pltpu.VMEM((32, 256), BF),
            pltpu.VMEM((32, 256), BF),
            pltpu.VMEM((256, 512), BF),
            pltpu.VMEM((256, 512), BF),
            pltpu.VMEM((2 * MX, C, Z), BF),
            pltpu.VMEM((NZ, 16, 128), BF),
            pltpu.VMEM((NZ, 16, 128), BF),
            pltpu.VMEM((NZ, 16, 128), BF),
            pltpu.VMEM((NZ, 16, 128), BF),
            pltpu.VMEM((NG, 32, 128), BF),
            pltpu.VMEM((NG, 32, 128), BF),
            pltpu.VMEM((NG, 32, 128), BF),
            pltpu.VMEM((NG, 32, 128), BF),
            pltpu.VMEM((32, 128), BF),
            pltpu.VMEM((NG, 32, 128), BF),
            pltpu.VMEM((NZ, 16, 128), BF),
            pltpu.VMEM((NB, 32, 128), BF),
            pltpu.VMEM((NB, 32, 128), BF),
            dma((14,)),
            dma((8,)),
            dma((8,)),
        ],
        compiler_params=pltpu.CompilerParams(
            collective_id=0, has_side_effects=True, vmem_limit_bytes=24 * 2**20
        ),
        cost_estimate=pl.CostEstimate(flops=10**9, bytes_accessed=4 * 2**20, transcendentals=0),
    )(*(pltpu.with_memory_space_constraint(a, pltpu.HBM) for a in operands))
    return pl.pallas_call(
        inverse_kernel,
        out_shape=(
            jax.ShapeDtypeStruct((1, 1, C, X, Z), BF),
            jax.ShapeDtypeStruct((2, MY, C, 2 * C), F32),
        ),
        in_specs=[vmem] * 4,
        out_specs=(anyw, anyw),
        scratch_shapes=[
            pltpu.VMEM((2 * MX, C, Z), F32),
            pltpu.VMEM((C, X, Z), BF),
            dma((5,)),
        ],
        compiler_params=pltpu.CompilerParams(vmem_limit_bytes=16 * 2**20),
        cost_estimate=pl.CostEstimate(flops=10**9, bytes_accessed=4 * 2**20, transcendentals=0),
    )(q, wg, zb, xb)


def solution(mesh):
    placed = (
        P("batch", "space", None, None, None),
        P("batch", "space", None, None, None),
        P("space", None, None, None),
    )
    return jax.shard_map(
        local,
        mesh=mesh,
        in_specs=placed,
        out_specs=(P("batch", "space", None, None, None), P("space", None, None, None)),
        check_vma=False,
    )
```

time: 85.4 us -> 42.2 us (0.49)
  the two profiles are of different devices: /device:TPU:1 before, /device:TPU:6 now
where the time goes in v1:
time: 42.2 us; the launch traced here: 42.1 us
  Pallas kernels  41.5 us (98%)
  between operations  0.67 us (2%)
    pallas_call x1, Pallas kernels, local(): pl.pallas_call(main_kernel, out_shape=(jax.ShapeDtypeStruct((NZ, 16, 128)...  39.7 us
    pallas_call x1, Pallas kernels, local(): pl.pallas_call(inverse_kernel, out_shape=(jax.ShapeDtypeStruct((1, 1, C,...  1.77 us

profile of v1, /device:TPU:6, one launch (start us, length us, event | category | flops | bytes accessed | tf_op | source)
XLA Modules:
  0.0 42.1 jit_solution(17790695594969391471)
XLA Ops:
  0.6 0.0 copy-start
  0.6 0.0 copy-start.1
  0.7 39.7 %shard_map.113 = (bf16[16,16,128]{2,1,0:T(8,128)(2,1)S(1)}, f32[2,16,64,128]{3,2,1,0:T(8,128)S(1)}) custom-call(bf16[1,1,64,64,128]{4,3,2,1,0:T(8,128)(2,1)} %in_hbm.1, bf16[1,1,64,64,128]{4,3,2,1,0:T(8,128)(2,1)} %cot_hbm.1, bf16[2,16,64,128]{3,2,1,0:T(8,128)(2,1)} %w_hbm.1, bf16[256,512]{1,0:T(8,128)(2,1)} %constant.14.clone.e8_hbm, ...), custom_call_target="tpu_custom_call" | custom-call | flops 1000000000 | bytes 4194304 | tf_op jit(solution)/shard_map/pallas_call | solution.py:311
  40.4 0.0 copy-done
  40.4 0.0 copy-done.1
  40.4 1.8 %shard_map.114 = (bf16[1,1,64,64,128]{4,3,2,1,0:T(8,128)(2,1)}, f32[2,16,64,128]{3,2,1,0:T(8,128)}) custom-call(bf16[16,16,128]{2,1,0:T(8,128)(2,1)S(1)} %get-tuple-element.4.q_ref, f32[2,16,64,128]{3,2,1,0:T(8,128)S(1)} %get-tuple-element.5.wg_ref, bf16[512,256]{1,0:T(8,128)(2,1)S(1)} %copy-done.1, bf16[512,256]{1,0:T(8,128)(2,1)S(1)} %copy-done), custom_call_target="tpu_custom_call" | custom-call | flops 1000000000 | bytes 4194304 | tf_op jit(solution)/shard_map/pallas_call | solution.py:351
Async XLA Ops:
  0.6 39.7 %copy-start = (bf16[512,256]{1,0:T(8,128)(2,1)S(1)}, bf16[512,256]{1,0:T(8,128)(2,1)}, u32[]{:S(2)}) copy-start(bf16[512,256]{1,0:T(8,128)(2,1)} %constant.20.clone.xb_ref) | copy-start | bytes 786436
  0.6 39.7 %copy-start.1 = (bf16[512,256]{1,0:T(8,128)(2,1)S(1)}, bf16[512,256]{1,0:T(8,128)(2,1)}, u32[]{:S(2)}) copy-start(bf16[512,256]{1,0:T(8,128)(2,1)} %constant.19.clone.zb_ref) | copy-start | bytes 786436
